TPU v7x, 32 devices: a whole 2x2x4 slice. The times are simulated.
32 devices in a mesh: ctx: 8 (over z, y), tp: 4 (over x, core).
Axes of the slice: x: 2, y: 2, z: 4, core: 2. Of those that a mesh axis runs over, the one named last changes fastest.
Arguments:
- features: bfloat16 [1024, 3, 4096], P('ctx', None, 'tp'), may hold values from -6 to 6
- short_taps: float32 [3, 3, 4096], P(None, None, 'tp'), may hold values from -3 to 3
- residues: float32 [16, 4096], P(None, 'tp'), may hold values from -2 to 2
- log_rate: float32 [16, 4096], P(None, 'tp'), may hold values from -13 to -3.5, as said below
- out_weight: bfloat16 [4096, 8192], P('tp'), may hold values from -0.09375 to 0.09375
- grad_out: bfloat16 [1024, 8192], P('ctx', 'tp'), may hold values from -6 to 6
Outputs:
- grad_features: bfloat16 [1024, 3, 4096], P('ctx', None, 'tp')
- grad_taps: float32 [3, 3, 4096], P(None, None, 'tp')
- grad_residues: float32 [16, 4096], P(None, 'tp')
- grad_log_rate: float32 [16, 4096], P(None, 'tp')
- grad_weight_t: float32 [8192, 4096], P('ctx', 'tp')
Inputs may be any that keep to these rules, and one draw needn't show every extreme that they name: `log_rate`: log of a decay rate per token.
All inputs are finite; a program needn't handle non-finite values.
Results may differ from a plain program's by a relative error of at most 0.0058.
Values may be sent and summed in bfloat16 or wider, within the bound.
A program may use at most 192 MiB of HBM per device.

v0:
```python
import jax
import jax.numpy as jnp
from jax import lax
from jax.sharding import PartitionSpec as P


def shifted(value, axis, steps):
    count = lax.axis_size(axis)
    first, last = (max(0, -steps), min(count, count - steps))
    return lax.ppermute(value, axis, [(source, source + steps) for source in range(first, last)])


def block_tables(residues, log_rate, block_len):
    decay_rate = jnp.exp(log_rate)
    amplitude = residues * jnp.exp(0.5 * log_rate)
    lag_steps = jnp.arange(block_len).astype(jnp.float32)
    kernel = jnp.sum(
        amplitude[:, None, :] * jnp.exp(-decay_rate[:, None, :] * lag_steps[None, :, None]), axis=0
    )
    row_ids = jnp.arange(block_len)[:, None]
    col_ids = jnp.arange(block_len)[None, :]
    distance = row_ids - col_ids
    toeplitz = jnp.where((distance >= 0)[:, :, None], kernel[jnp.maximum(distance, 0)], 0.0)
    injection = jnp.exp(-decay_rate[:, None, :] * (block_len - 1 - lag_steps)[None, :, None])
    readout = amplitude[:, None, :] * jnp.exp(
        -decay_rate[:, None, :] * (lag_steps + 1.0)[None, :, None]
    )
    return (decay_rate, toeplitz, injection, readout)


def combine_states(earlier, later):
    return (earlier[0] * later[0], later[0] * earlier[1] + later[1])


def long_conv(product, residues, log_rate):
    block_len = 128
    length, channels = product.shape
    block_count = length // block_len
    decay_rate, toeplitz, injection, readout = block_tables(residues, log_rate, block_len)
    blocks = product.reshape(block_count, block_len, channels)
    inside = jnp.einsum("ijc,bjc->bic", toeplitz, blocks, precision=lax.Precision.HIGHEST)
    entering = jnp.einsum("rjc,bjc->brc", injection, blocks, precision=lax.Precision.HIGHEST)
    carry_decay = jnp.broadcast_to(jnp.exp(-decay_rate * block_len), entering.shape)
    unused, states = lax.associative_scan(combine_states, (carry_decay, entering), axis=0)
    before = jnp.concatenate([jnp.zeros_like(states[:1]), states[:-1]], axis=0)
    from_past = jnp.einsum("ric,brc->bic", readout, before, precision=lax.Precision.HIGHEST)
    return (inside + from_past).reshape(length, channels)


def to_channels(values):
    return lax.all_to_all(values, "ctx", split_axis=1, concat_axis=0, tiled=True)


def to_tokens(values):
    return lax.all_to_all(values, "ctx", split_axis=0, concat_axis=1, tiled=True)


def per_device(features, short_taps, residues, log_rate, out_weight, grad_out):
    length = features.shape[0]
    tap_count = short_taps.shape[0]
    groups = lax.axis_size("ctx")
    position = lax.axis_index("ctx")
    rim_rows = shifted(features[length - (tap_count - 1) :], "ctx", 1)
    padded_in = jnp.concatenate([rim_rows, features], axis=0).astype(jnp.float32)
    shortened = sum(
        (
            short_taps[lag] * padded_in[tap_count - 1 - lag : tap_count - 1 - lag + length]
            for lag in range(tap_count)
        )
    )
    product = (shortened[:, 1] * shortened[:, 2]).astype(jnp.bfloat16)
    chan_width = product.shape[1] // groups
    local_residues = lax.dynamic_slice_in_dim(residues, position * chan_width, chan_width, 1)
    local_rates = lax.dynamic_slice_in_dim(log_rate, position * chan_width, chan_width, 1)
    product_chan = to_channels(product).astype(jnp.float32)
    conv_chan, pullback = jax.vjp(long_conv, product_chan, local_residues, local_rates)
    convolved = to_tokens(conv_chan.astype(jnp.bfloat16)).astype(jnp.float32)
    gated = (shortened[:, 0] * convolved).astype(jnp.bfloat16)
    cotangent = lax.all_gather(grad_out, "tp", axis=1, tiled=True)
    grad_weight_t = lax.psum_scatter(
        lax.dot_general(
            cotangent, gated, (((0,), (0,)), ((), ())), preferred_element_type=jnp.float32
        ),
        "ctx",
        scatter_dimension=0,
        tiled=True,
    )
    grad_gated = lax.dot_general(
        cotangent, out_weight, (((1,), (1,)), ((), ())), preferred_element_type=jnp.float32
    )
    grad_conv = (grad_gated * shortened[:, 0]).astype(jnp.bfloat16)
    grad_prod_chan, grad_res_local, grad_rate_local = pullback(
        to_channels(grad_conv).astype(jnp.float32)
    )
    grad_product = to_tokens(grad_prod_chan.astype(jnp.bfloat16)).astype(jnp.float32)
    grad_residues, grad_log_rate = (
        lax.all_gather(grad_res_local, "ctx", axis=1, tiled=True),
        lax.all_gather(grad_rate_local, "ctx", axis=1, tiled=True),
    )
    grad_short = jnp.stack(
        [grad_gated * convolved, grad_product * shortened[:, 2], grad_product * shortened[:, 1]],
        axis=1,
    )
    tail_rows = shifted(grad_short[: tap_count - 1], "ctx", -1)
    tail_pad = jnp.concatenate([grad_short, tail_rows], axis=0)
    grad_features = sum(
        (short_taps[lag] * tail_pad[lag : lag + length] for lag in range(tap_count))
    )
    partial_taps = jnp.stack(
        [
            jnp.sum(
                grad_short * padded_in[tap_count - 1 - lag : tap_count - 1 - lag + length], axis=0
            )
            for lag in range(tap_count)
        ],
        axis=0,
    )
    grad_taps = lax.psum(partial_taps, "ctx")
    return (
        grad_features.astype(jnp.bfloat16),
        grad_taps,
        grad_residues,
        grad_log_rate,
        grad_weight_t,
    )


def solution(mesh):
    return jax.shard_map(
        per_device,
        mesh=mesh,
        in_specs=(
            P("ctx", None, "tp"),
            P(None, None, "tp"),
            P(None, "tp"),
            P(None, "tp"),
            P("tp", None),
            P("ctx", "tp"),
        ),
        out_specs=(
            P("ctx", None, "tp"),
            P(None, None, "tp"),
            P(None, "tp"),
            P(None, "tp"),
            P("ctx", "tp"),
        ),
        check_vma=False,
    )
```

profile of v0, /device:TPU:0, one launch (start us, length us, event | category | flops | bytes accessed | tf_op | source)
XLA Modules:
  0.0 879.5 jit_solution(6375209423134570061)
XLA Ops:
  8.7 4.9 collective-permute-start
  16.3 1.4 maximum_convert_fusion
  18.9 1.8 copy.151
  20.7 5.3 all-to-all-start
  28.0 6.5 all-to-all-done
  34.5 2.8 fusion.16
  37.4 1.2 copy.128
  38.6 13.0 %multiply_convert_fusion.1 = (bf16[128,1024]{1,0:T(8,128)(2,1)}, f32[128,1024]{1,0:T(8,128)}) fusion(f32[128,3,1024]{2,0,1:T(8,128)S(1)} %multiply_add_fusion, bf16[128,8192]{1,0:T(8,128)(2,1)} %all-gather.2.cloned.1.call-done, bf16[1024,8192]{1,0:T(8,128)(2,1)} %param.10), kind=kOutput, calls=%fused_computation.43 | convolution fusion | flops 2147745792 | bytes 20185088 | tf_op jit(solution)/shard_map/dot_general | solution.py:88
  51.6 1.8 copy.153
  53.4 4.1 all-to-all-start.2
  60.4 3.2 pad.240
  63.6 2.0 all-to-all-done.2
  65.7 3.0 fusion.11
  68.7 1.8 copy.134
  72.0 1.3 pad_maximum_fusion.3
  73.3 1.8 pad.157
  76.0 1.0 copy.156
  77.0 3.3 fusion.13
  80.3 5.6 select_bitcast_fusion
  85.9 9.3 %copy.155 = f32[128,128,128]{2,1,0:T(8,128)} copy(f32[128,128,128]{1,0,2:T(8,128)} %select_bitcast_fusion) | data formatting | bytes 16777216 | tf_op jit(solution)/shard_map/transpose(jvp(jit(_where)))/select_n | solution.py:23
  95.2 98.8 %scatter_custom_fusion = f32[128,128]{1,0:T(8,128)S(1)} fusion(s32[16384]{0:T(1024)} %maximum_bitcast_fusion, f32[16384,128]{1,0:T(8,128)} %bitcast.83, f32[]{:T(128)} %constant.7.clone.1), kind=kCustom, calls=%fused_computation.85 | custom fusion | flops 2097152 | bytes 66048 | tf_op jit(solution)/shard_map/transpose(jvp())/scatter-add | solution.py:23
  194.8 4.6 multiply_reduce_fusion.4
  200.3 54.8 %gather_fusion = f32[16384,128]{1,0:T(8,128)} fusion(f32[128,128]{1,0:T(8,128)S(1)} %copy.124, s32[16384]{0:T(1024)S(1)} %broadcast_clamp_fusion), kind=kCustom, calls=%fused_computation | custom fusion | bytes 16842752 | tf_op jit(solution)/shard_map/jvp()/gather | solution.py:23
  255.1 9.9 %broadcast_select_fusion = f32[128,128,128]{2,1,0:T(8,128)} fusion(f32[128,128,128]{2,1,0:T(8,128)} %bitcast.82, pred[128,128]{1,0:T(8,128)(4,1)} %subtract_compare_fusion), kind=kLoop, calls=%fused_computation.4 | loop fusion | flops 2097152 | bytes 16793600 | tf_op jit(solution)/shard_map/jvp(jit(_where))/select_n | solution.py:23
  265.1 9.3 %copy.126 = f32[128,128,128]{1,0,2:T(8,128)} copy(f32[128,128,128]{2,1,0:T(8,128)} %broadcast_select_fusion) | data formatting | bytes 16777216 | tf_op jit(solution)/shard_map/jvp(jit(_where))/select_n | solution.py:23
  274.3 10.1 %fusion.9 = bf16[8,128,128]{1,0,2:T(8,128)(2,1)S(1)} fusion(f32[128,8,128]{2,1,0:T(8,128)} %fusion.13, f32[128,128,128]{1,0,2:T(8,128)} %copy.126, bf16[128,8,128]{0,2,1:T(8,128)(2,1)} %all-to-all-done), kind=kOutput, calls=%fused_computation.26 | convolution fusion | flops 201588736 | bytes 9437184 | tf_op jit(solution)/shard_map/jvp(ijc,bjc->bic)/dot_general | solution.py:41
  284.5 12.0 %all_to_all.43 = bf16[8,128,128]{1,2,0:T(8,128)(2,1)S(1)} all-to-all(bf16[8,128,128]{1,2,0:T(8,128)(2,1)S(1)} %copy.130), channel_id=1, replica_groups=mesh['ctx'=8,'tp'=4] {'ctx'}, dimensions={0} | all-to-all | bytes 524288 | tf_op jit(solution)/shard_map/all_to_all | solution.py:55
  297.3 2.0 copy.152
  299.4 17.4 %convolution_bitcast_fusion = f32[8192,1024]{0,1:T(8,128)} fusion(bf16[128,8192]{1,0:T(8,128)(2,1)} %all-gather.2.cloned.1.call-done, f32[128,1024]{1,0:T(8,128)} %copy.152, f32[128,3,1024]{2,0,1:T(8,128)S(1)} %multiply_add_fusion), kind=kOutput, calls=%fused_computation.2 | convolution fusion | flops 2147745792 | bytes 36700160 | tf_op jit(solution)/shard_map/dot_general | solution.py:81
  316.8 1.3 split.21
  320.3 1.9 pad.134
  322.2 1.4 multiply_add_fusion.1
  323.8 2.6 pad.113
  327.3 1.0 copy.135
  328.3 2.2 fusion.15
  330.5 7.5 fusion.8
  338.7 4.1 all-to-all-start.3
  342.8 3.3 fusion.5
  351.6 32.6 %all_gather.11 = f32[16,1024]{1,0:T(8,128)S(1)} all-gather(f32[16,128]{1,0:T(8,128)S(1)} %get-tuple-element.56), channel_id=1, replica_groups=mesh['ctx'=8,'tp'=4] {'ctx'}, dimensions={1}, use_global_device_ids=true | all-gather | bytes 73728 | tf_op jit(solution)/shard_map/all_gather | solution.py:98
  384.2 1.8 convert_element_type.104
  386.0 2.0 copy.154
  388.0 1.3 multiply_bitcast_fusion
  389.6 1.3 collective-permute-start.1
  391.0 32.0 %all_gather.10 = f32[16,1024]{1,0:T(8,128)S(1)} all-gather(f32[16,128]{1,0:T(8,128)S(1)} %get-tuple-element.57), channel_id=1, replica_groups=mesh['ctx'=8,'tp'=4] {'ctx'}, dimensions={1}, use_global_device_ids=true | all-gather | bytes 73728 | tf_op jit(solution)/shard_map/all_gather | solution.py:97
  423.2 1.9 multiply_reduce_fusion.2
  425.1 40.6 %psum.7 = f32[3,3,1024]{2,1,0:T(4,128)} all-reduce(f32[3,3,1024]{2,1,0:T(4,128)S(1)} %pad_maximum_fusion.2), channel_id=1, replica_groups=mesh['ctx'=8,'tp'=4] {'ctx'}, use_global_device_ids=true, to_apply=%region_4.5 | all-reduce | flops 9216 | bytes 73728 | tf_op jit(solution)/shard_map/psum | solution.py:118
  465.8 400.1 %reduce-scatter.2.cloned.1.call-done = f32[1024,1024]{0,1:T(8,128)} async-done(((f32[8192,1024]{0,1:T(8,128)}), f32[1024,1024]{0,1:T(8,128)}) %reduce-scatter.2.cloned.1.call-update) | async-done | bytes 4194320 | tf_op jit(solution)/shard_map/reduce_scatter | solution.py:80
  865.8 5.3 copy.150
  (119 shorter events, 26.1 us)
Async XLA Ops:
  7.2 31.5 %all-gather.2.cloned.1.call-start = ((), (), s32[]{:S(2)}) async-start(), calls=%async_computation.5 | async-start | bytes 2621440 | tf_op jit(solution)/shard_map/all_gather | solution.py:79
  8.7 7.6 collective-permute-start
  13.6 20.9 %copy-start.20 = (f32[128]{0:T(128)}, f32[128]{0:T(128)S(1)}, u32[]{:S(2)}) copy-start(f32[128]{0:T(128)S(1)} %broadcast_subtract_fusion) | copy-start | bytes 1540
  15.0 23.6 %copy-start.15 = (f32[16,128]{1,0:T(8,128)}, f32[16,128]{1,0:T(8,128)S(1)}, u32[]{:S(2)}) copy-start(f32[16,128]{1,0:T(8,128)S(1)} %get-tuple-element.51) | copy-start | bytes 24580
  15.8 2.4 copy-start.3
  15.8 2.4 copy-start.5
  15.8 2.4 copy-start.7
  20.7 13.8 %all-to-all-start = ((bf16[128,8,128]{0,2,1:T(8,128)(2,1)}), bf16[128,8,128]{0,2,1:T(8,128)(2,1)}, u32[]{:S(2)}, u32[]{:S(2)}) async-start(bf16[128,8,128]{0,2,1:T(8,128)(2,1)} %bitcast.87), calls=%async_computation | async-start | bytes 524288 | tf_op jit(solution)/shard_map/all_to_all | solution.py:51
  38.6 19.2 %copy-start.17 = (f32[2,16,128]{2,1,0:T(8,128)}, f32[2,16,128]{2,1,0:T(8,128)S(1)}, u32[]{:S(2)}) copy-start(f32[2,16,128]{2,1,0:T(8,128)S(1)} %slice_add_fusion.3) | copy-start | bytes 49156
  53.4 12.3 %all-to-all-start.2 = ((bf16[128,8,128]{0,2,1:T(8,128)(2,1)}), bf16[128,8,128]{0,2,1:T(8,128)(2,1)}, u32[]{:S(2)}, u32[]{:S(2)}) async-start(bf16[128,8,128]{0,2,1:T(8,128)(2,1)} %bitcast.86), calls=%async_computation.2 | async-start | bytes 524288 | tf_op jit(solution)/shard_map/all_to_all | solution.py:51
  57.5 808.4 %reduce-scatter.2.cloned.1.call-start = ((), (), s32[]{:S(2)}) async-start(), calls=%async_computation.6 | async-start | bytes 37748736 | tf_op jit(solution)/shard_map/reduce_scatter | solution.py:80
  57.8 0.6 copy-start.11
  57.8 0.6 copy-start.13
  71.4 2.0 copy-start.10
  77.0 3.3 copy-start.2
  316.8 1.4 copy-start.1
  316.8 1.4 copy-start.12
  316.8 1.4 copy-start.14
  316.8 2.0 copy-start.18
  316.8 2.0 copy-start.16
  316.8 2.0 copy-start.22
  330.5 12.3 %copy-start.21 = (f32[128]{0:T(128)S(1)}, f32[128]{0:T(128)}, u32[]{:S(2)}) copy-start(f32[128]{0:T(128)} %copy-done.20) | copy-start | bytes 1540
  338.0 8.2 copy-start.19
  338.0 8.2 copy-start.9
  338.7 45.5 %all-to-all-start.3 = ((bf16[8,128,128]{1,2,0:T(8,128)(2,1)}), bf16[8,128,128]{1,2,0:T(8,128)(2,1)}, u32[]{:S(2)}, u32[]{:S(2)}) async-start(bf16[8,128,128]{1,2,0:T(8,128)(2,1)} %copy.137), calls=%async_computation.3 | async-start | bytes 524288 | tf_op jit(solution)/shard_map/all_to_all | solution.py:55
  388.0 1.4 copy-start
  389.6 33.3 %collective-permute-start.1 = (f32[2,3,1024]{2,0,1:T(2,128)S(1)}, f32[2,3,1024]{2,0,1:T(2,128)S(1)}, u32[]{:S(2)}, u32[]{:S(2)}) collective-permute-start(f32[2,3,1024]{2,0,1:T(2,128)S(1)} %slice.179), channel_id=1, source_target_pairs={{4,0},{8,4},{12,8},{16,12},{20,16},{24,20},{28,24},{5,1},{9,5},{13... | collective-permute-start | bytes 73736 | tf_op jit(solution)/shard_map/ppermute | solution.py:10
  390.9 32.3 %copy-start.4 = (f32[3,1024]{1,0:T(4,128)S(1)}, f32[3,1024]{1,0:T(4,128)}, u32[]{:S(2)}) copy-start(f32[3,1024]{1,0:T(4,128)} %copy-done.3) | copy-start | bytes 36868
  390.9 32.3 %copy-start.6 = (f32[3,1024]{1,0:T(4,128)S(1)}, f32[3,1024]{1,0:T(4,128)}, u32[]{:S(2)}) copy-start(f32[3,1024]{1,0:T(4,128)} %copy-done.5) | copy-start | bytes 36868
  390.9 32.3 %copy-start.8 = (f32[3,1024]{1,0:T(4,128)S(1)}, f32[3,1024]{1,0:T(4,128)}, u32[]{:S(2)}) copy-start(f32[3,1024]{1,0:T(4,128)} %copy-done.7) | copy-start | bytes 36868
Sparse Core Ops, SparseCore 0:
  9.6 25.2 all-gather.1
  317.0 548.8 reduce-scatter.1
where the time goes:
time: 888 us; the launch traced here: 879 us
  waiting for transfers between devices  409 us (46%)
  other arithmetic  129 us (15%)
  blocking collectives  117 us (13%)
  local copies, waits for them, and re-layouts  116 us (13%)
  matrix products  72.8 us (8%)
  starting transfers between devices  20 us (2%)
  between operations  14.8 us (2%)
    reduce_scatter x1, waiting for transfers between devices, per_device(): lax.psum_scatter(lax.dot_general(cotangent, gated, (((0,), (0,)), ((), ()...  400 us
    scatter-add x1, other arithmetic, block_tables(): kernel[jnp.maximum(distance, 0)]  98.8 us
    gather x1, local copies, waits for them, and re-layouts, block_tables(): kernel[jnp.maximum(distance, 0)]  54.8 us
    psum x1, blocking collectives, per_device(): grad_taps = lax.psum(partial_taps, 'ctx')  40.6 us
    all_gather x1, blocking collectives, per_device(): lax.all_gather(grad_rate_local, 'ctx', axis=1, tiled=True)  32.6 us
    all_gather x1, blocking collectives, per_device(): lax.all_gather(grad_res_local, 'ctx', axis=1, tiled=True)  32 us
    dot_general x3, matrix products, long_conv(): jnp.einsum('ijc,bjc->bic', toeplitz, blocks, precision=lax.Precision.HIGH...  23.2 us
    select_n x2, local copies, waits for them, and re-layouts, block_tables(): jnp.where((distance >= 0)[:, :, None], kernel[jnp.maximum(distance, 0)],...  18.6 us
  transfers between devices with their start and end apart: 7, of which 3 were waited for; matrix products, arithmetic and copies ran while one was open for 7% of the time, Pallas kernels for 0%

commit v1 on v0

--- a/solution.py
+++ b/solution.py
@@ -115,7 +115,11 @@
         ],
         axis=0,
     )
-    grad_taps = lax.psum(partial_taps, "ctx")
+    grad_taps = partial_taps
+    for hop in (1, 2, 4):
+        grad_taps = grad_taps + lax.ppermute(
+            grad_taps, "ctx", [(dev, dev ^ hop) for dev in range(8)]
+        )
     return (
         grad_features.astype(jnp.bfloat16),
         grad_taps,

time: 888 us -> 888 us (level)
  waiting for transfers between devices: 409 us -> 434 us
  blocking collectives: 117 us -> 94.6 us
    psum x1 -> x0, blocking collectives: 40.6 us -> none  [per_device(): grad_taps = lax.psum(partial_taps, 'ctx')]
    all_to_all x1 -> x2, blocking collectives: 12 us -> 31.2 us  [to_tokens(): lax.all_to_all(values, 'ctx', split_axis=0, concat_axis=1, tiled=True)]
    reduce_scatter x1, waiting for transfers between devices: 400 us -> 418 us  [per_device(): lax.psum_scatter(lax.dot_general(cotangent, gated, (((0,), (0,)), ((), ()...]
  transfers between devices with their start and end apart: 7 -> 9, of which waited for: 3 -> 5; matrix products, arithmetic and copies ran while one was open for 7% -> 6% of each run, Pallas kernels for 0% -> 0%
where the time goes in v1:
time: 888 us; the launch traced here: 881 us
  waiting for transfers between devices  434 us (49%)
  other arithmetic  130 us (15%)
  local copies, waits for them, and re-layouts  115 us (13%)
  blocking collectives  94.6 us (11%)
  matrix products  72.6 us (8%)
  starting transfers between devices  19.3 us (2%)
  between operations  14.9 us (2%)
    reduce_scatter x1, waiting for transfers between devices, per_device(): lax.psum_scatter(lax.dot_general(cotangent, gated, (((0,), (0,)), ((), ()...  418 us
    scatter-add x1, other arithmetic, block_tables(): kernel[jnp.maximum(distance, 0)]  98.8 us
    gather x1, local copies, waits for them, and re-layouts, block_tables(): kernel[jnp.maximum(distance, 0)]  54.8 us
    all_gather x1, blocking collectives, per_device(): lax.all_gather(grad_rate_local, 'ctx', axis=1, tiled=True)  31.8 us
    all_gather x1, blocking collectives, per_device(): lax.all_gather(grad_res_local, 'ctx', axis=1, tiled=True)  31.6 us
    all_to_all x2, blocking collectives, to_tokens(): lax.all_to_all(values, 'ctx', split_axis=0, concat_axis=1, tiled=True)  31.2 us
    dot_general x3, matrix products, long_conv(): jnp.einsum('ijc,bjc->bic', toeplitz, blocks, precision=lax.Precision.HIGH...  23.2 us
    select_n x2, local copies, waits for them, and re-layouts, block_tables(): jnp.where((distance >= 0)[:, :, None], kernel[jnp.maximum(distance, 0)],...  18.7 us
  transfers between devices with their start and end apart: 9, of which 5 were waited for; matrix products, arithmetic and copies ran while one was open for 6% of the time, Pallas kernels for 0%

profile of v1, /device:TPU:0, one launch (start us, length us, event | category | flops | bytes accessed | tf_op | source)
XLA Modules:
  0.0 880.6 jit_solution(10229562988520164522)
XLA Ops:
  8.7 4.9 collective-permute-start
  16.4 1.4 maximum_convert_fusion
  19.0 1.8 copy.151
  20.8 5.2 all-to-all-start
  28.1 6.5 all-to-all-done
  34.6 2.8 fusion.16
  37.5 1.2 copy.128
  38.7 13.0 %multiply_convert_fusion.1 = (bf16[128,1024]{1,0:T(8,128)(2,1)}, f32[128,1024]{1,0:T(8,128)}) fusion(f32[128,3,1024]{2,0,1:T(8,128)S(1)} %multiply_add_fusion, bf16[128,8192]{1,0:T(8,128)(2,1)} %all-gather.2.cloned.1.call-done, bf16[1024,8192]{1,0:T(8,128)(2,1)} %param.10), kind=kOutput, calls=%fused_computation.43 | convolution fusion | flops 2147745792 | bytes 20185088 | tf_op jit(solution)/shard_map/dot_general | solution.py:88
  51.7 1.8 copy.153
  53.5 4.1 all-to-all-start.2
  60.5 3.2 pad.246
  63.7 2.0 all-to-all-done.2
  65.8 3.0 fusion.11
  68.8 1.8 copy.134
  72.1 1.3 pad_maximum_fusion.3
  73.5 1.8 pad.157
  77.1 3.3 fusion.13
  80.4 5.6 select_bitcast_fusion
  86.0 9.4 %copy.155 = f32[128,128,128]{2,1,0:T(8,128)} copy(f32[128,128,128]{1,0,2:T(8,128)} %select_bitcast_fusion) | data formatting | bytes 16777216 | tf_op jit(solution)/shard_map/transpose(jvp(jit(_where)))/select_n | solution.py:23
  95.4 98.8 %scatter_custom_fusion = f32[128,128]{1,0:T(8,128)S(1)} fusion(s32[16384]{0:T(1024)} %maximum_bitcast_fusion, f32[16384,128]{1,0:T(8,128)} %bitcast.83, f32[]{:T(128)} %constant.7.clone.1), kind=kCustom, calls=%fused_computation.85 | custom fusion | flops 2097152 | bytes 66048 | tf_op jit(solution)/shard_map/transpose(jvp())/scatter-add | solution.py:23
  194.9 4.6 multiply_reduce_fusion.4
  200.5 54.8 %gather_fusion = f32[16384,128]{1,0:T(8,128)} fusion(f32[128,128]{1,0:T(8,128)S(1)} %copy.124, s32[16384]{0:T(1024)S(1)} %broadcast_clamp_fusion), kind=kCustom, calls=%fused_computation | custom fusion | bytes 16842752 | tf_op jit(solution)/shard_map/jvp()/gather | solution.py:23
  255.3 10.0 %broadcast_select_fusion = f32[128,128,128]{2,1,0:T(8,128)} fusion(f32[128,128,128]{2,1,0:T(8,128)} %bitcast.82, pred[128,128]{1,0:T(8,128)(4,1)} %subtract_compare_fusion), kind=kLoop, calls=%fused_computation.4 | loop fusion | flops 2097152 | bytes 16793600 | tf_op jit(solution)/shard_map/jvp(jit(_where))/select_n | solution.py:23
  265.3 9.3 %copy.126 = f32[128,128,128]{1,0,2:T(8,128)} copy(f32[128,128,128]{2,1,0:T(8,128)} %broadcast_select_fusion) | data formatting | bytes 16777216 | tf_op jit(solution)/shard_map/jvp(jit(_where))/select_n | solution.py:23
  274.6 10.1 %fusion.9 = bf16[8,128,128]{1,0,2:T(8,128)(2,1)S(1)} fusion(f32[128,8,128]{2,1,0:T(8,128)} %fusion.13, f32[128,128,128]{1,0,2:T(8,128)} %copy.126, bf16[128,8,128]{0,2,1:T(8,128)(2,1)} %all-to-all-done), kind=kOutput, calls=%fused_computation.26 | convolution fusion | flops 201588736 | bytes 9437184 | tf_op jit(solution)/shard_map/jvp(ijc,bjc->bic)/dot_general | solution.py:41
  284.7 12.0 %all_to_all.43 = bf16[8,128,128]{1,2,0:T(8,128)(2,1)S(1)} all-to-all(bf16[8,128,128]{1,2,0:T(8,128)(2,1)S(1)} %copy.130), channel_id=1, replica_groups=mesh['ctx'=8,'tp'=4] {'ctx'}, dimensions={0} | all-to-all | bytes 524288 | tf_op jit(solution)/shard_map/all_to_all | solution.py:55
  297.5 2.0 copy.152
  299.6 17.4 %convolution_bitcast_fusion = f32[8192,1024]{0,1:T(8,128)} fusion(bf16[128,8192]{1,0:T(8,128)(2,1)} %all-gather.2.cloned.1.call-done, f32[128,1024]{1,0:T(8,128)} %copy.152, f32[128,3,1024]{2,0,1:T(8,128)S(1)} %multiply_add_fusion), kind=kOutput, calls=%fused_computation.2 | convolution fusion | flops 2147745792 | bytes 36700160 | tf_op jit(solution)/shard_map/dot_general | solution.py:81
  317.0 1.3 split.21
  320.4 1.4 multiply_add_fusion.1
  321.9 2.6 pad.113
  325.4 1.0 copy.135
  326.4 2.2 fusion.15
  328.6 7.5 fusion.8
  336.2 19.2 %all_to_all.44 = bf16[8,128,128]{1,2,0:T(8,128)(2,1)S(1)} all-to-all(bf16[8,128,128]{1,2,0:T(8,128)(2,1)S(1)} %copy.137), channel_id=1, replica_groups=mesh['ctx'=8,'tp'=4] {'ctx'}, dimensions={0} | all-to-all | bytes 524288 | tf_op jit(solution)/shard_map/all_to_all | solution.py:55
  356.2 2.0 copy.154
  358.2 1.3 multiply_bitcast_fusion
  361.0 1.6 collective-permute-start.1
  362.6 3.2 fusion.5
  366.0 1.3 collective-permute-done.1
  367.4 1.4 pad_maximum_fusion
  368.8 1.9 multiply_reduce_fusion.2
  370.7 3.0 collective-permute-start.2
  379.2 5.8 collective-permute-done.3
  385.0 31.8 %all_gather.11 = f32[16,1024]{1,0:T(8,128)S(1)} all-gather(f32[16,128]{1,0:T(8,128)S(1)} %get-tuple-element.56), channel_id=1, replica_groups=mesh['ctx'=8,'tp'=4] {'ctx'}, dimensions={1}, use_global_device_ids=true | all-gather | bytes 73728 | tf_op jit(solution)/shard_map/all_gather | solution.py:98
  416.8 31.6 %all_gather.10 = f32[16,1024]{1,0:T(8,128)S(1)} all-gather(f32[16,128]{1,0:T(8,128)S(1)} %get-tuple-element.57), channel_id=1, replica_groups=mesh['ctx'=8,'tp'=4] {'ctx'}, dimensions={1}, use_global_device_ids=true | all-gather | bytes 73728 | tf_op jit(solution)/shard_map/all_gather | solution.py:97
  449.1 417.8 %reduce-scatter.2.cloned.1.call-done = f32[1024,1024]{0,1:T(8,128)} async-done(((f32[8192,1024]{0,1:T(8,128)}), f32[1024,1024]{0,1:T(8,128)}) %reduce-scatter.2.cloned.1.call-update) | async-done | bytes 4194320 | tf_op jit(solution)/shard_map/reduce_scatter | solution.py:80
  866.9 5.3 copy.150
  (142 shorter events, 29.2 us)
Async XLA Ops:
  7.2 31.6 %all-gather.2.cloned.1.call-start = ((), (), s32[]{:S(2)}) async-start(), calls=%async_computation.5 | async-start | bytes 2621440 | tf_op jit(solution)/shard_map/all_gather | solution.py:79
  8.7 7.7 collective-permute-start
  13.6 21.0 %copy-start.28 = (f32[128]{0:T(128)}, f32[128]{0:T(128)S(1)}, u32[]{:S(2)}) copy-start(f32[128]{0:T(128)S(1)} %broadcast_subtract_fusion) | copy-start | bytes 1540
  15.0 23.7 %copy-start.23 = (f32[16,128]{1,0:T(8,128)}, f32[16,128]{1,0:T(8,128)S(1)}, u32[]{:S(2)}) copy-start(f32[16,128]{1,0:T(8,128)S(1)} %get-tuple-element.51) | copy-start | bytes 24580
  15.8 2.5 copy-start.10
  15.8 2.5 copy-start.12
  15.8 2.5 copy-start.14
  20.8 13.8 %all-to-all-start = ((bf16[128,8,128]{0,2,1:T(8,128)(2,1)}), bf16[128,8,128]{0,2,1:T(8,128)(2,1)}, u32[]{:S(2)}, u32[]{:S(2)}) async-start(bf16[128,8,128]{0,2,1:T(8,128)(2,1)} %bitcast.87), calls=%async_computation | async-start | bytes 524288 | tf_op jit(solution)/shard_map/all_to_all | solution.py:51
  38.7 19.2 %copy-start.25 = (f32[2,16,128]{2,1,0:T(8,128)}, f32[2,16,128]{2,1,0:T(8,128)S(1)}, u32[]{:S(2)}) copy-start(f32[2,16,128]{2,1,0:T(8,128)S(1)} %slice_add_fusion.3) | copy-start | bytes 49156
  53.5 12.3 %all-to-all-start.2 = ((bf16[128,8,128]{0,2,1:T(8,128)(2,1)}), bf16[128,8,128]{0,2,1:T(8,128)(2,1)}, u32[]{:S(2)}, u32[]{:S(2)}) async-start(bf16[128,8,128]{0,2,1:T(8,128)(2,1)} %bitcast.86), calls=%async_computation.2 | async-start | bytes 524288 | tf_op jit(solution)/shard_map/all_to_all | solution.py:51
  57.5 809.4 %reduce-scatter.2.cloned.1.call-start = ((), (), s32[]{:S(2)}) async-start(), calls=%async_computation.6 | async-start | bytes 37748736 | tf_op jit(solution)/shard_map/reduce_scatter | solution.py:80
  57.9 0.6 copy-start.19
  57.9 0.6 copy-start.21
  71.5 2.0 copy-start.18
  77.1 3.3 copy-start.9
  317.0 1.4 copy-start.8
  317.0 1.4 copy-start.20
  317.0 1.4 copy-start.22
  317.0 2.0 copy-start.26
  317.0 2.0 copy-start.24
  317.0 2.0 copy-start.30
  358.2 1.4 copy-start.6
  359.6 0.8 copy-start
  359.7 6.1 copy-start.2
  359.7 6.1 copy-start.4
  359.7 2.9 copy-start.7
  359.7 2.9 copy-start.29
  360.4 5.5 copy-start.27
  360.4 5.5 copy-start.17
  360.4 5.6 copy-start.16
  361.0 6.4 copy-start.1
  361.0 6.4 collective-permute-start.1
  365.9 2.8 copy-start.3
  365.9 2.8 copy-start.5
  366.0 2.8 copy-start.11
  366.0 2.8 copy-start.13
  366.0 2.8 copy-start.15
  370.7 7.6 collective-permute-start.2
  378.3 6.6 collective-permute-start.3
  384.9 63.5 %collective-permute-start.4 = (f32[3,3,1024]{2,1,0:T(4,128)S(1)}, f32[3,3,1024]{2,1,0:T(4,128)S(1)}, u32[]{:S(2)}, u32[]{:S(2)}) collective-permute-start(f32[3,3,1024]{2,1,0:T(4,128)S(1)} %fusion.68), channel_id=1, source_target_pairs={{0,16},{4,20},{8,24},{12,28},{16,0},{20,4},{24,8},{28,12},{1,17},{... | collective-permute-start | bytes 110600 | tf_op jit(solution)/shard_map/ppermute | solution.py:120
Sparse Core Ops, SparseCore 0:
  9.6 25.2 all-gather.1
  317.2 549.7 reduce-scatter.1
